TPU v7x, 256 devices: a whole 4x4x8 slice. The times are simulated.
256 devices in a mesh: dp: 16 (over z_lo, y, core), feat: 16 (over x, z_hi).
Axes of the slice: x: 4, y: 4, z: 8 (z_hi: 4, z_lo: 2; z = z_hi * 2 + z_lo), core: 2. Of those that a mesh axis runs over, the one named last changes fastest.
Arguments:
- images: bfloat16 [6144, 3072], P('dp'), may hold values from -6 to 6
- labels: int32 [6144], P('dp'), may hold values from 0 to 9
- frequencies: bfloat16 [3072, 16384], P(None, 'feat'), may hold values from -0.15625 to 0.15625
- privacy_noise: float32 [10, 2, 16384], P(None, None, 'feat'), may hold values from -0.6 to 0.6
- latents: bfloat16 [4096, 256], P('dp'), may hold values from -6 to 6
- gen_labels: int32 [4096], P('dp'), may hold values from 0 to 9
- gen_in: bfloat16 [256, 1024], replicated, may hold values from -0.375 to 0.375
- gen_out: bfloat16 [1024, 3072], replicated, may hold values from -0.25 to 0.25
Outputs:
- match_loss: float32 [], replicated
- grad_in: float32 [256, 1024], P('dp')
- grad_out: float32 [1024, 3072], P('dp')
All inputs are finite; a program needn't handle non-finite values.
Results may differ from a plain program's by a relative error of at most 0.0035.
Values sent between devices are 32-bit elements; how exact they have to be, the bound alone decides.
A program may use at most 128 MiB of HBM per device.

v0:
```python
import jax
import jax.numpy as jnp
from jax import lax
from jax.sharding import PartitionSpec as P


def class_sums(phase, classes_of, classes, scale):
    feats = jnp.concatenate([jnp.cos(phase), jnp.sin(phase)], axis=1)
    onehot = (classes_of[:, None] == jnp.arange(classes)[None, :]).astype(jnp.float32)
    sums = jnp.dot(onehot.T, feats, precision=lax.Precision.HIGHEST) * scale
    return (sums.reshape(classes, 2, phase.shape[1]), onehot)


def generator_grads(image_grad, image_out, hidden, pre_hidden, sigmoid_h, latents, gen_out):
    out_grad = (image_grad * (1.0 - image_out * image_out)).astype(jnp.bfloat16)
    grad_out = jnp.einsum("gh,gd->hd", hidden, out_grad, preferred_element_type=jnp.float32)
    back_hidden = jnp.einsum("gd,hd->gh", out_grad, gen_out, preferred_element_type=jnp.float32)
    hidden_grad = (back_hidden * sigmoid_h * (1.0 + pre_hidden * (1.0 - sigmoid_h))).astype(
        jnp.bfloat16
    )
    grad_in = jnp.einsum("gz,gh->zh", latents, hidden_grad, preferred_element_type=jnp.float32)
    return (grad_in, grad_out)


def per_device(images, labels, frequencies, privacy_noise, latents, gen_labels, gen_in, gen_out):
    classes = privacy_noise.shape[0]
    feat_dev = frequencies.shape[1]
    data_devices = lax.axis_size("dp")
    feat_devices = lax.axis_size("feat")
    total_images = images.shape[0] * data_devices
    total_gen = latents.shape[0] * data_devices
    total_feats = feat_dev * feat_devices
    data_phase = jnp.dot(images, frequencies, preferred_element_type=jnp.float32)
    data_part, unused = class_sums(data_phase, labels, classes, classes / total_images)
    pre_hidden = jnp.dot(latents, gen_in, preferred_element_type=jnp.float32)
    sigmoid_h = jax.nn.sigmoid(pre_hidden)
    hidden = (pre_hidden * sigmoid_h).astype(jnp.bfloat16)
    image_out = jnp.tanh(jnp.dot(hidden, gen_out, preferred_element_type=jnp.float32))
    gen_image = image_out.astype(jnp.bfloat16)
    gen_phase = jnp.dot(gen_image, frequencies, preferred_element_type=jnp.float32)
    gen_part, gen_onehot = class_sums(gen_phase, gen_labels, classes, classes / total_gen)
    shares = lax.psum_scatter(data_part, "dp", scatter_dimension=2, tiled=True)
    share_width = feat_dev // data_devices
    noisy = shares + lax.dynamic_slice_in_dim(
        privacy_noise, lax.axis_index("dp") * share_width, share_width, 2
    )
    released = lax.all_gather(noisy, "dp", axis=2, tiled=True)
    mean_gap = lax.psum(gen_part, "dp") - released
    match_loss = lax.psum(jnp.sum(mean_gap * mean_gap), "feat") / (2.0 * total_feats)
    gap_rows = jnp.dot(
        gen_onehot, mean_gap.reshape(classes, 2 * feat_dev), precision=lax.Precision.HIGHEST
    ) * (16.0 * classes / total_gen)
    phase_grad = (
        jnp.cos(gen_phase) * gap_rows[:, feat_dev:] - jnp.sin(gen_phase) * gap_rows[:, :feat_dev]
    ).astype(jnp.bfloat16)
    partial_image = jnp.einsum(
        "gf,df->gd", phase_grad, frequencies, preferred_element_type=jnp.float32
    )
    image_grad = lax.psum(partial_image, "feat")
    grad_in, grad_out = generator_grads(
        image_grad, image_out, hidden, pre_hidden, sigmoid_h, latents, gen_out
    )
    grad_in, grad_out = (
        lax.psum_scatter(grad_in, "dp", scatter_dimension=0, tiled=True),
        lax.psum_scatter(grad_out, "dp", scatter_dimension=0, tiled=True),
    )
    return (match_loss, grad_in, grad_out)


def solution(mesh):
    return jax.shard_map(
        per_device,
        mesh=mesh,
        in_specs=(
            P("dp", None),
            P("dp"),
            P(None, "feat"),
            P(None, None, "feat"),
            P("dp", None),
            P("dp"),
            P(),
            P(),
        ),
        out_specs=(P(), P("dp", None), P("dp", None)),
        check_vma=False,
    )
```

profile of v0, /device:TPU:2, one launch (start us, length us, event | category | flops | bytes accessed | tf_op | source)
XLA Modules:
  0.0 608.0 jit_solution(4414337173241759052)
XLA Ops:
  7.2 0.0 copy-start
  7.2 0.0 reduce-scatter.10.cloned.1.call-start
  7.2 1.6 copy-done
  8.8 12.2 %fusion.29 = (f32[384,1024]{1,0:T(8,128)S(1)}, f32[384,1024]{1,0:T(8,128)S(1)}) fusion(bf16[384,3072]{1,0:T(8,128)(2,1)S(1)} %copy-done, bf16[3072,1024]{1,0:T(8,128)(2,1)} %param.10), kind=kOutput, calls=%fused_computation.40 | convolution fusion | flops 2415919104 | bytes 11796480 | tf_op jit(solution)/shard_map/dot_general | solution.py:33
  21.0 1.2 fusion.4
  22.2 0.1 reshape.18
  22.3 5.8 copy.19
  28.1 6.3 %reshape.20 = f32[1024,20]{1,0:T(8,128)} reshape(f32[1024,10,2]{2,1,0:T(8,128)} %bitcast.20) | data formatting | bytes 163840
  34.4 0.0 reduce-scatter.10.cloned.1.call-update
  34.4 0.0 all-reduce.3.cloned.1.call-start
  34.5 0.0 slice-start
  34.5 0.3 fusion.31
  34.8 1.0 copy-done.4
  35.8 5.0 convolution_tanh_fusion
  40.8 0.0 copy-start.9
  40.8 5.3 fusion.30
  46.1 1.0 copy-done.2
  47.1 0.8 convolution_multiply_fusion.1
  48.0 0.7 reshape.17
  48.7 2.0 copy.15
  50.7 0.0 all-reduce.3.cloned.1.call-update
  50.7 0.2 all-reduce.5.cloned.1.call-start
  51.0 49.8 %reduce-scatter.10.cloned.1.call-done = f32[64,20]{1,0:T(8,128)} async-done(((f32[1024,20]{1,0:T(8,128)}), f32[64,20]{1,0:T(8,128)}) %reduce-scatter.10.cloned.1.call-update) | async-done | bytes 5136
  100.7 1.8 reshape.21
  102.5 1.2 copy.20
  103.7 0.8 dynamic-slice_add_fusion
  104.5 0.1 copy.16
  104.6 21.0 %all_gather.3 = f32[10,2,1024]{0,1,2:T(2,128)} all-gather(f32[10,2,64]{0,1,2:T(2,128)S(1)} %copy.16), channel_id=1, replica_groups=mesh['dp'=16,'feat'=16] {'dp'}, dimensions={2}, use_global_device_ids=true | all-gather | bytes 87040 | tf_op jit(solution)/shard_map/all_gather | solution.py:47
  125.6 100.2 %all-reduce.3.cloned.1.call-done = f32[10,2,1024]{0,1,2:T(2,128)} async-done(((f32[10,2,1024]{0,1,2:T(2,128)}), f32[10,2,1024]{0,1,2:T(2,128)}) %all-reduce.3.cloned.1.call-update) | async-done | bytes 81936 | tf_op jit(solution)/shard_map/psum | solution.py:48
  225.8 4.1 multiply_reduce_fusion
  229.9 1.4 copy.17
  231.4 1.0 convolution_multiply_fusion
  232.5 0.1 copy-done.3
  232.6 6.5 %fusion.19 = f32[256,3072]{1,0:T(8,128)} fusion(bf16[3072,1024]{1,0:T(8,128)(2,1)} %param.10, f32[256,1024]{1,0:T(8,128)S(1)} %copy-done.3, f32[256,2048]{1,0:T(8,128)S(1)} %convolution_multiply_fusion, f32[256,1024]{1,0:T(8,128)S(1)} %get-tuple-element.16), kind=kOutput, calls=%fused_computation.28 | convolution fusion | flops 1611661312 | bytes 13631488 | tf_op jit(solution)/shard_map/gf,df->gd/dot_general | solution.py:56
  239.0 0.0 all-reduce.5.cloned.1.call-update
  239.1 0.0 copy-start.8
  239.1 0.0 reduce-scatter.12.cloned.1.call-start
  239.1 197.6 %all-reduce.5.cloned.1.call-done = f32[256,3072]{1,0:T(8,128)} async-done(((f32[256,3072]{1,0:T(8,128)}), f32[256,3072]{1,0:T(8,128)}) %all-reduce.5.cloned.1.call-update) | async-done | bytes 3145744 | tf_op jit(solution)/shard_map/psum | solution.py:59
  436.7 4.6 multiply_convert_fusion
  441.3 6.6 %convolution_bitcast_fusion = f32[256,1024]{0,1:T(8,128)} fusion(bf16[256,256]{1,0:T(8,128)(2,1)S(1)} %copy-done.8, bf16[256,3072]{1,0:T(8,128)(2,1)} %multiply_convert_fusion, bf16[1024,3072]{1,0:T(8,128)(2,1)} %param.15, f32[256,1024]{1,0:T(8,128)S(1)} %copy-done.5), kind=kOutput, calls=%fused_computation.16 | convolution fusion | flops 1747189760 | bytes 10092544 | tf_op jit(solution)/shard_map/gz,gh->zh/dot_general | solution.py:21
  447.9 2.5 copy.21
  450.4 0.0 reduce-scatter.12.cloned.1.call-update
  450.4 0.0 reduce-scatter.8.cloned.1.call-start
  450.5 7.8 %fusion.28 = f32[1024,3072]{1,0:T(8,128)} fusion(bf16[256,3072]{1,0:T(8,128)(2,1)} %multiply_convert_fusion, f32[256,1024]{1,0:T(8,128)S(1)} %copy-done.5), kind=kOutput, calls=%fused_computation.39 | convolution fusion | flops 1611923456 | bytes 15204352 | tf_op jit(solution)/shard_map/gh,gd->hd/dot_general | solution.py:16
  458.3 0.0 reduce-scatter.8.cloned.1.call-update
  458.3 41.1 %psum.22 = f32[]{:T(128)} all-reduce(f32[]{:T(128)} %get-tuple-element.12), channel_id=1, replica_groups=mesh['dp'=16,'feat'=16] {'feat'}, use_global_device_ids=true, to_apply=%region_3.0 | all-reduce | flops 1 | bytes 8 | tf_op jit(solution)/shard_map/psum | solution.py:49
  500.0 14.2 %reduce-scatter.12.cloned.1.call-done = f32[16,1024]{1,0:T(8,128)} async-done(((f32[256,1024]{1,0:T(8,128)}), f32[16,1024]{1,0:T(8,128)}) %reduce-scatter.12.cloned.1.call-update) | async-done | bytes 65552
  514.3 86.1 %reduce-scatter.8.cloned.1.call-done = f32[64,3072]{1,0:T(8,128)} async-done(((f32[1024,3072]{1,0:T(8,128)}), f32[64,3072]{1,0:T(8,128)}) %reduce-scatter.8.cloned.1.call-update) | async-done | bytes 786448 | tf_op jit(solution)/shard_map/reduce_scatter | solution.py:65
  (21 shorter events, 0.1 us)
Async XLA Ops:
  7.2 1.7 copy-start
  7.2 13.8 %copy-start.10 = (s32[384]{0:T(512)S(1)}, s32[384]{0:T(512)}, u32[]{:S(2)}) copy-start(s32[384]{0:T(512)} %param.9) | copy-start | bytes 4612
  7.2 93.6 %reduce-scatter.10.cloned.1.call-start = ((), (), s32[]{:S(2)}) async-start(), calls=%async_computation.6 | async-start | bytes 557056
  28.1 6.4 %copy-start.6 = (bf16[256,1024]{1,0:T(8,128)(2,1)S(1)}, bf16[256,1024]{1,0:T(8,128)(2,1)}, u32[]{:S(2)}) copy-start(bf16[256,1024]{1,0:T(8,128)(2,1)} %param.14) | copy-start | bytes 1572868
  28.1 6.4 %copy-start.7 = (bf16[256,256]{1,0:T(8,128)(2,1)S(1)}, bf16[256,256]{1,0:T(8,128)(2,1)}, u32[]{:S(2)}) copy-start(bf16[256,256]{1,0:T(8,128)(2,1)} %param.12) | copy-start | bytes 393220
  34.4 191.3 %all-reduce.3.cloned.1.call-start = ((), (), s32[]{:S(2)}) async-start(), calls=%async_computation.3 | async-start | bytes 2097152 | tf_op jit(solution)/shard_map/psum | solution.py:48
  34.5 6.3 %slice-start = ((s8[6291456]{0:T(1024)(128)(4,1)}), s8[4194304]{0:T(1024)(128)(4,1)S(1)}, s32[]{:S(2)}) async-start(s8[6291456]{0:T(1024)(128)(4,1)} %bitcast.21), calls=%async_computation.8 | async-start | bytes 8388608
  34.8 1.0 copy-start.4
  35.8 5.0 slice-start.1
  40.8 5.3 copy-start.1
  40.8 6.3 %copy-start.9 = (s32[256]{0:T(256)S(1)}, s32[256]{0:T(256)}, u32[]{:S(2)}) copy-start(s32[256]{0:T(256)} %param.13) | copy-start | bytes 3076
  46.1 1.0 copy-start.2
  50.7 386.0 %all-reduce.5.cloned.1.call-start = ((), (), s32[]{:S(2)}) async-start(), calls=%async_computation.4 | async-start | bytes 6291456 | tf_op jit(solution)/shard_map/psum | solution.py:59
  231.3 1.2 copy-start.3
  239.1 202.3 %copy-start.5 = (f32[256,1024]{1,0:T(8,128)S(1)}, f32[256,1024]{1,0:T(8,128)}, u32[]{:S(2)}) copy-start(f32[256,1024]{1,0:T(8,128)} %copy-done.4) | copy-start | bytes 3145732
  239.1 202.3 %copy-start.8 = (bf16[256,256]{1,0:T(8,128)(2,1)S(1)}, bf16[256,256]{1,0:T(8,128)(2,1)}, u32[]{:S(2)}) copy-start(bf16[256,256]{1,0:T(8,128)(2,1)} %param.12) | copy-start | bytes 393220
  239.1 275.2 %reduce-scatter.12.cloned.1.call-start = ((), (), s32[]{:S(2)}) async-start(), calls=%async_computation.7 | async-start | bytes 1114112
  450.4 150.0 %reduce-scatter.8.cloned.1.call-start = ((), (), s32[]{:S(2)}) async-start(), calls=%async_computation.5 | async-start | bytes 13369344 | tf_op jit(solution)/shard_map/reduce_scatter | solution.py:65
Sparse Core Ops, SparseCore 0:
  34.5 66.1 reduce-scatter.9
  103.6 122.1 all-reduce.2
  239.2 197.4 all-reduce.4
  450.5 63.6 reduce-scatter.11
  517.4 82.9 reduce-scatter.7
where the time goes:
time: 609 us; the launch traced here: 608 us
  waiting for transfers between devices  448 us (74%)
  blocking collectives  62.1 us (10%)
  matrix products  46.6 us (8%)
  local copies, waits for them, and re-layouts  25.8 us (4%)
  between operations  15.8 us (3%)
  other arithmetic  9.52 us (2%)
    psum x1, waiting for transfers between devices, per_device(): image_grad = lax.psum(partial_image, 'feat')  198 us
    psum x1, waiting for transfers between devices, per_device(): mean_gap = lax.psum(gen_part, 'dp') - released  100 us
    reduce_scatter x1, waiting for transfers between devices, per_device(): lax.psum_scatter(grad_out, 'dp', scatter_dimension=0, tiled=True)  86.1 us
    unnamed x7, waiting for transfers between devices  64.1 us
    psum x1, blocking collectives, per_device(): lax.psum(jnp.sum(mean_gap * mean_gap), 'feat') / (2.0 * total_feats)  41.1 us
    unnamed x33, local copies, waits for them, and re-layouts  21.4 us
    all_gather x1, blocking collectives, per_device(): released = lax.all_gather(noisy, 'dp', axis=2, tiled=True)  21 us
  transfers between devices with their start and end apart: 5, of which 5 were waited for; matrix products, arithmetic and copies ran while one was open for 4% of the time, Pallas kernels for 0%

commit v1 on v0

--- a/solution.py
+++ b/solution.py
@@ -45,7 +45,7 @@
         privacy_noise, lax.axis_index("dp") * share_width, share_width, 2
     )
     released = lax.all_gather(noisy, "dp", axis=2, tiled=True)
-    mean_gap = lax.psum(gen_part, "dp") - released
+    mean_gap = jnp.sum(lax.all_gather(gen_part, "dp"), axis=0) - released
     match_loss = lax.psum(jnp.sum(mean_gap * mean_gap), "feat") / (2.0 * total_feats)
     gap_rows = jnp.dot(
         gen_onehot, mean_gap.reshape(classes, 2 * feat_dev), precision=lax.Precision.HIGHEST

time: 609 us -> 517 us (0.85)
  waiting for transfers between devices: 448 us -> 358 us
    psum x1 -> x0, waiting for transfers between devices: 100 us -> none  [per_device(): mean_gap = lax.psum(gen_part, 'dp') - released]
    all_gather x0 -> x1, waiting for transfers between devices: none -> 8.68 us  [per_device(): mean_gap = jnp.sum(lax.all_gather(gen_part, 'dp'), axis=0) - released]
  transfers between devices with their start and end apart: 5 -> 5, of which waited for: 5 -> 5; matrix products, arithmetic and copies ran while one was open for 4% -> 5% of each run, Pallas kernels for 0% -> 0%
where the time goes in v1:
time: 517 us; the launch traced here: 516 us
  waiting for transfers between devices  358 us (69%)
  blocking collectives  62.7 us (12%)
  matrix products  46.6 us (9%)
  local copies, waits for them, and re-layouts  23.6 us (5%)
  between operations  15.8 us (3%)
  other arithmetic  9.43 us (2%)
    psum x1, waiting for transfers between devices, per_device(): image_grad = lax.psum(partial_image, 'feat')  197 us
    reduce_scatter x1, waiting for transfers between devices, per_device(): lax.psum_scatter(grad_out, 'dp', scatter_dimension=0, tiled=True)  86 us
    unnamed x7, waiting for transfers between devices  66.1 us
    psum x1, blocking collectives, per_device(): lax.psum(jnp.sum(mean_gap * mean_gap), 'feat') / (2.0 * total_feats)  41.1 us
    all_gather x1, blocking collectives, per_device(): released = lax.all_gather(noisy, 'dp', axis=2, tiled=True)  21.6 us
    unnamed x33, local copies, waits for them, and re-layouts  21.3 us
    dot_general x1, matrix products, per_device(): jnp.dot(images, frequencies, preferred_element_type=jnp.float32)  12.2 us
  transfers between devices with their start and end apart: 5, of which 5 were waited for; matrix products, arithmetic and copies ran while one was open for 5% of the time, Pallas kernels for 0%

profile of v1, /device:TPU:2, one launch (start us, length us, event | category | flops | bytes accessed | tf_op | source)
XLA Modules:
  0.0 516.0 jit_solution(1172709336957919192)
XLA Ops:
  7.2 0.0 copy-start
  7.2 0.0 reduce-scatter.10.cloned.1.call-start
  7.2 1.6 copy-done
  8.8 12.2 %fusion.29 = (f32[384,1024]{1,0:T(8,128)S(1)}, f32[384,1024]{1,0:T(8,128)S(1)}) fusion(bf16[384,3072]{1,0:T(8,128)(2,1)S(1)} %copy-done, bf16[3072,1024]{1,0:T(8,128)(2,1)} %param.10), kind=kOutput, calls=%fused_computation.40 | convolution fusion | flops 2415919104 | bytes 11796480 | tf_op jit(solution)/shard_map/dot_general | solution.py:33
  21.0 1.2 fusion.4
  22.2 0.1 reshape.14
  22.3 5.8 %copy.20 = f32[10,2,1024]{1,0,2:T(8,128)} copy(f32[10,2,1024]{2,1,0:T(2,128)S(1)} %reshape.14) | data formatting | bytes 163840
  28.1 6.3 %reshape.16 = f32[1024,20]{1,0:T(8,128)} reshape(f32[1024,10,2]{2,1,0:T(8,128)} %bitcast.20) | data formatting | bytes 163840
  34.4 0.0 reduce-scatter.10.cloned.1.call-update
  34.4 0.0 all-gather.2.cloned.1.call-start
  34.5 0.0 slice-start
  34.5 0.3 fusion.31
  34.8 1.0 copy-done.4
  35.8 5.0 convolution_tanh_fusion
  40.8 0.0 copy-start.9
  40.8 5.3 %fusion.30 = (f32[256,1024]{1,0:T(8,128)S(1)}, f32[256,1024]{1,0:T(8,128)S(1)}) fusion(bf16[3072,1024]{1,0:T(8,128)(2,1)S(1)} %bitcast.22, f32[256,3072]{1,0:T(8,128)S(1)} %convolution_tanh_fusion), kind=kOutput, calls=%fused_computation.41 | convolution fusion | flops 1611399168 | bytes 11534336 | tf_op jit(solution)/shard_map/dot_general | solution.py:40
  46.1 1.0 copy-done.2
  47.2 0.0 copy-done.9
  47.2 0.8 convolution_multiply_fusion.1
  48.0 0.7 all_gather_reshape.3
  48.7 0.0 all-gather.2.cloned.1.call-update
  48.7 0.2 all-reduce.2.cloned.1.call-start
  49.0 51.8 %reduce-scatter.10.cloned.1.call-done = f32[64,20]{1,0:T(8,128)} async-done(((f32[1024,20]{1,0:T(8,128)}), f32[64,20]{1,0:T(8,128)}) %reduce-scatter.10.cloned.1.call-update) | async-done | bytes 5136
  100.7 1.8 reshape.17
  102.5 1.2 copy.21
  103.7 0.8 dynamic-slice_add_fusion
  104.5 0.1 copy.17
  104.6 21.6 %all_gather.7 = f32[10,2,1024]{0,1,2:T(2,128)} all-gather(f32[10,2,64]{0,1,2:T(2,128)S(1)} %copy.17), channel_id=1, replica_groups=mesh['dp'=16,'feat'=16] {'dp'}, dimensions={2}, use_global_device_ids=true | all-gather | bytes 87040 | tf_op jit(solution)/shard_map/all_gather | solution.py:47
  126.2 1.4 copy.18
  127.6 8.7 %all-gather.2.cloned.1.call-done = f32[16,10,2,1024]{3,2,1,0:T(2,128)} async-done(((f32[1,10,2,1024]{3,2,1,0:T(2,128)}), f32[16,10,2,1024]{3,2,1,0:T(2,128)}) %all-gather.2.cloned.1.call-update) | async-done | bytes 1310736 | tf_op jit(solution)/shard_map/all_gather | solution.py:48
  136.3 2.4 reduce_sum.18
  138.7 1.7 multiply_reduce_fusion
  140.5 1.0 convolution_multiply_fusion
  141.5 6.5 %fusion.19 = f32[256,3072]{1,0:T(8,128)} fusion(bf16[3072,1024]{1,0:T(8,128)(2,1)} %param.10, f32[256,1024]{1,0:T(8,128)S(1)} %copy-done.3, f32[256,2048]{1,0:T(8,128)S(1)} %convolution_multiply_fusion, f32[256,1024]{1,0:T(8,128)S(1)} %get-tuple-element.19), kind=kOutput, calls=%fused_computation.27 | convolution fusion | flops 1611661312 | bytes 13631488 | tf_op jit(solution)/shard_map/gf,df->gd/dot_general | solution.py:56
  148.0 0.0 all-reduce.2.cloned.1.call-update
  148.0 0.0 copy-start.8
  148.0 0.0 reduce-scatter.12.cloned.1.call-start
  148.1 196.8 %all-reduce.2.cloned.1.call-done = f32[256,3072]{1,0:T(8,128)} async-done(((f32[256,3072]{1,0:T(8,128)}), f32[256,3072]{1,0:T(8,128)}) %all-reduce.2.cloned.1.call-update) | async-done | bytes 3145744 | tf_op jit(solution)/shard_map/psum | solution.py:59
  344.8 4.6 multiply_convert_fusion
  349.4 6.6 %convolution_bitcast_fusion = f32[256,1024]{0,1:T(8,128)} fusion(bf16[256,256]{1,0:T(8,128)(2,1)S(1)} %copy-done.8, bf16[256,3072]{1,0:T(8,128)(2,1)} %multiply_convert_fusion, bf16[1024,3072]{1,0:T(8,128)(2,1)} %param.15, f32[256,1024]{1,0:T(8,128)S(1)} %copy-done.5), kind=kOutput, calls=%fused_computation.16 | convolution fusion | flops 1747189760 | bytes 10092544 | tf_op jit(solution)/shard_map/gz,gh->zh/dot_general | solution.py:21
  356.0 2.5 copy.22
  358.5 0.0 reduce-scatter.12.cloned.1.call-update
  358.6 0.0 reduce-scatter.8.cloned.1.call-start
  358.6 7.8 %fusion.28 = f32[1024,3072]{1,0:T(8,128)} fusion(bf16[256,3072]{1,0:T(8,128)(2,1)} %multiply_convert_fusion, f32[256,1024]{1,0:T(8,128)S(1)} %copy-done.5), kind=kOutput, calls=%fused_computation.39 | convolution fusion | flops 1611923456 | bytes 15204352 | tf_op jit(solution)/shard_map/gh,gd->hd/dot_general | solution.py:16
  366.4 0.0 reduce-scatter.8.cloned.1.call-update
  366.4 41.1 %psum.14 = f32[]{:T(128)} all-reduce(f32[]{:T(128)} %get-tuple-element.15), channel_id=1, replica_groups=mesh['dp'=16,'feat'=16] {'feat'}, use_global_device_ids=true, to_apply=%region_3.0 | all-reduce | flops 1 | bytes 8 | tf_op jit(solution)/shard_map/psum | solution.py:49
  408.2 14.2 %reduce-scatter.12.cloned.1.call-done = f32[16,1024]{1,0:T(8,128)} async-done(((f32[256,1024]{1,0:T(8,128)}), f32[16,1024]{1,0:T(8,128)}) %reduce-scatter.12.cloned.1.call-update) | async-done | bytes 65552
  422.4 86.0 %reduce-scatter.8.cloned.1.call-done = f32[64,3072]{1,0:T(8,128)} async-done(((f32[1024,3072]{1,0:T(8,128)}), f32[64,3072]{1,0:T(8,128)}) %reduce-scatter.8.cloned.1.call-update) | async-done | bytes 786448 | tf_op jit(solution)/shard_map/reduce_scatter | solution.py:65
  (21 shorter events, 0.1 us)
Async XLA Ops:
  7.2 1.7 copy-start
  7.2 13.8 %copy-start.10 = (s32[384]{0:T(512)S(1)}, s32[384]{0:T(512)}, u32[]{:S(2)}) copy-start(s32[384]{0:T(512)} %param.9) | copy-start | bytes 4612
  7.2 93.6 %reduce-scatter.10.cloned.1.call-start = ((), (), s32[]{:S(2)}) async-start(), calls=%async_computation.6 | async-start | bytes 557056
  28.1 6.4 %copy-start.6 = (bf16[256,1024]{1,0:T(8,128)(2,1)S(1)}, bf16[256,1024]{1,0:T(8,128)(2,1)}, u32[]{:S(2)}) copy-start(bf16[256,1024]{1,0:T(8,128)(2,1)} %param.14) | copy-start | bytes 1572868
  28.1 6.4 %copy-start.7 = (bf16[256,256]{1,0:T(8,128)(2,1)S(1)}, bf16[256,256]{1,0:T(8,128)(2,1)}, u32[]{:S(2)}) copy-start(bf16[256,256]{1,0:T(8,128)(2,1)} %param.12) | copy-start | bytes 393220
  34.4 101.9 %all-gather.2.cloned.1.call-start = ((), (), s32[]{:S(2)}) async-start(), calls=%async_computation.3 | async-start | bytes 1392640 | tf_op jit(solution)/shard_map/all_gather | solution.py:48
  34.5 6.3 %slice-start = ((s8[6291456]{0:T(1024)(128)(4,1)}), s8[4194304]{0:T(1024)(128)(4,1)S(1)}, s32[]{:S(2)}) async-start(s8[6291456]{0:T(1024)(128)(4,1)} %bitcast.21), calls=%async_computation.8 | async-start | bytes 8388608
  34.8 1.0 copy-start.4
  35.8 5.0 slice-start.1
  40.8 5.3 %copy-start.1 = (f32[256,3072]{1,0:T(8,128)}, f32[256,3072]{1,0:T(8,128)S(1)}, u32[]{:S(2)}) copy-start(f32[256,3072]{1,0:T(8,128)S(1)} %convolution_tanh_fusion) | copy-start | bytes 9437188
  40.8 6.3 %copy-start.9 = (s32[256]{0:T(256)S(1)}, s32[256]{0:T(256)}, u32[]{:S(2)}) copy-start(s32[256]{0:T(256)} %param.13) | copy-start | bytes 3076
  46.1 1.0 copy-start.2
  48.7 296.1 %all-reduce.2.cloned.1.call-start = ((), (), s32[]{:S(2)}) async-start(), calls=%async_computation.4 | async-start | bytes 6291456 | tf_op jit(solution)/shard_map/psum | solution.py:59
  138.7 2.8 copy-start.3
  148.0 201.5 %copy-start.5 = (f32[256,1024]{1,0:T(8,128)S(1)}, f32[256,1024]{1,0:T(8,128)}, u32[]{:S(2)}) copy-start(f32[256,1024]{1,0:T(8,128)} %copy-done.4) | copy-start | bytes 3145732
  148.0 201.4 %copy-start.8 = (bf16[256,256]{1,0:T(8,128)(2,1)S(1)}, bf16[256,256]{1,0:T(8,128)(2,1)}, u32[]{:S(2)}) copy-start(bf16[256,256]{1,0:T(8,128)(2,1)} %param.12) | copy-start | bytes 393220
  148.0 274.4 %reduce-scatter.12.cloned.1.call-start = ((), (), s32[]{:S(2)}) async-start(), calls=%async_computation.7 | async-start | bytes 1114112
  358.6 149.8 %reduce-scatter.8.cloned.1.call-start = ((), (), s32[]{:S(2)}) async-start(), calls=%async_computation.5 | async-start | bytes 13369344 | tf_op jit(solution)/shard_map/reduce_scatter | solution.py:65
Sparse Core Ops, SparseCore 0:
  34.5 66.1 reduce-scatter.9
  102.7 33.5 all-gather.1
  148.1 196.6 all-reduce.1
  358.7 63.6 reduce-scatter.11
  425.4 82.9 reduce-scatter.7
